TPU v7x, 128 devices: a whole 4x4x4 slice. The times are simulated.
128 devices in a mesh: ctx: 32 (over y, x, z_lo), tp: 4 (over z_hi, core).
Axes of the slice: x: 4, y: 4, z: 4 (z_hi: 2, z_lo: 2; z = z_hi * 2 + z_lo), core: 2. Of those that a mesh axis runs over, the one named last changes fastest.
Arguments:
- streams: bfloat16 [3, 4096, 65536], P(None, 'tp', 'ctx'), parts along dimension 1, may hold values from -6 to 6
- short_filters: float32 [3, 3, 4096], P(None, None, 'tp'), parts along dimension 2, may hold values from -3 to 3
- residues: float32 [16, 4096], P(None, 'tp'), parts along dimension 1, may hold values from -1 to 1
- rates: float32 [16, 4096], P(None, 'tp'), parts along dimension 1, may hold values from 3.0517579e-06 to 0.05
- skip: float32 [4096], P('tp'), parts along dimension 0, may hold values from 0.5 to 1.5
Outputs:
- output: bfloat16 [4096, 65536], P('tp', 'ctx'), parts along dimension 0
There are 4 independent parts, one for each index of `tp`. A program takes and returns all parts, laid end to end along the dimension named above; each array names one. Nothing has to cross between parts.
All inputs are finite; a program needn't handle non-finite values.
Results may differ from a plain program's by a relative error of at most 0.0064.
Values may be sent and summed in bfloat16 or wider, within the bound.
No kernel may reach another device: no remote copies, remote signals or barrier semaphores. Data moves between devices by JAX's collectives and lax.ppermute only.
A program may use at most 192 MiB of HBM per device.

v0:
```python
import math

import jax
import jax.numpy as jnp
from jax import lax
from jax.sharding import PartitionSpec as P

SHORT = 3


PRECISE = lax.Precision.HIGH


def shifted(shard, axis, by):
    devices = lax.axis_size(axis)
    pairs = [(i, i + by) for i in range(devices) if 0 <= i + by < devices]
    return lax.ppermute(shard, axis, pairs)


def angle_table(row_count, col_count, modulus):
    row_index = jnp.arange(row_count, dtype=jnp.int32)[:, None]
    col_index = jnp.arange(col_count, dtype=jnp.int32)[None, :]
    phase = (row_index * col_index % modulus).astype(jnp.float32) * (2.0 * math.pi / modulus)
    return (jnp.cos(phase), -jnp.sin(phase))


def forward_spectrum(signal, tables):
    first_re, first_im, twist_re, twist_im, second_re, second_im = tables
    part_re = jnp.einsum("kh,ghn->gkn", first_re, signal, precision=PRECISE)
    part_im = jnp.einsum("kh,ghn->gkn", first_im, signal, precision=PRECISE)
    turned_re = part_re * twist_re - part_im * twist_im
    turned_im = part_re * twist_im + part_im * twist_re
    spec_re = jnp.einsum("gkn,nm->gkm", turned_re, second_re, precision=PRECISE) - jnp.einsum(
        "gkn,nm->gkm", turned_im, second_im, precision=PRECISE
    )
    spec_im = jnp.einsum("gkn,nm->gkm", turned_re, second_im, precision=PRECISE) + jnp.einsum(
        "gkn,nm->gkm", turned_im, second_re, precision=PRECISE
    )
    return (spec_re, spec_im)


def inverse_first_half(spec_re, spec_im, tables, modulus):
    first_re, first_im, twist_re, twist_im, second_re, second_im = tables
    back_re = jnp.einsum("gkm,mn->gkn", spec_re, second_re, precision=PRECISE) + jnp.einsum(
        "gkm,mn->gkn", spec_im, second_im, precision=PRECISE
    )
    back_im = jnp.einsum("gkm,mn->gkn", spec_im, second_re, precision=PRECISE) - jnp.einsum(
        "gkm,mn->gkn", spec_re, second_im, precision=PRECISE
    )
    turned_re = back_re * twist_re + back_im * twist_im
    turned_im = back_im * twist_re - back_re * twist_im
    result = jnp.einsum("kh,gkn->ghn", first_re, turned_re, precision=PRECISE) + jnp.einsum(
        "kh,gkn->ghn", first_im, turned_im, precision=PRECISE
    )
    return result / float(modulus)


def long_conv(gated_chan, residues, rates, skip):
    channels, length = gated_chan.shape
    modulus = 2 * length
    cols = 128
    row_full = modulus // cols
    row_half = row_full // 2
    first_re, first_im = angle_table(row_full, row_half, row_full)
    twist_re, twist_im = angle_table(row_full, cols, modulus)
    second_re, second_im = angle_table(cols, cols, cols)
    tables = (first_re, first_im, twist_re, twist_im, second_re, second_im)
    positions = jnp.arange(length, dtype=jnp.float32)
    group = 8
    blocks = channels // group

    def one_block(items):
        gated_block, residue_block, rate_block, skip_block = items
        long_filter = jnp.sum(
            (residue_block * jnp.sqrt(2.0 * rate_block))[:, :, None]
            * jnp.exp(-rate_block[:, :, None] * positions[None, None, :]),
            axis=0,
        )
        signal = gated_block.astype(jnp.float32)
        data_re, data_im = forward_spectrum(signal.reshape(group, row_half, cols), tables)
        kern_re, kern_im = forward_spectrum(long_filter.reshape(group, row_half, cols), tables)
        prod_re = data_re * kern_re - data_im * kern_im
        prod_im = data_re * kern_im + data_im * kern_re
        conv = inverse_first_half(prod_re, prod_im, tables, modulus).reshape(group, length)
        return (conv + skip_block[:, None] * signal).astype(jnp.bfloat16)

    gated_blocks = gated_chan.reshape(blocks, group, length)
    residue_blocks = jnp.transpose(residues.reshape(residues.shape[0], blocks, group), (1, 0, 2))
    rate_blocks = jnp.transpose(rates.reshape(rates.shape[0], blocks, group), (1, 0, 2))
    skip_blocks = skip.reshape(blocks, group)
    mixed = lax.map(one_block, (gated_blocks, residue_blocks, rate_blocks, skip_blocks))
    return mixed.reshape(channels, length)


def on_device(streams, short_filters, residues, rates, skip):
    local_len = streams.shape[2]
    rims = shifted(streams[:, :, local_len - (SHORT - 1) :], "ctx", 1)
    extended = jnp.concatenate([rims, streams], axis=2)
    filtered = jnp.zeros(streams.shape, jnp.float32)
    for offset in range(SHORT):
        begin = SHORT - 1 - offset
        filtered = filtered + short_filters[:, offset, :, None] * extended[
            :, :, begin : begin + local_len
        ].astype(jnp.float32)
    gated = (filtered[1] * filtered[2]).astype(jnp.bfloat16)
    query = filtered[0].astype(jnp.bfloat16)
    per_device = streams.shape[1] // lax.axis_size("ctx")
    first_channel = lax.axis_index("ctx") * per_device
    own_residues = lax.dynamic_slice_in_dim(residues, first_channel, per_device, 1)
    own_rates = lax.dynamic_slice_in_dim(rates, first_channel, per_device, 1)
    own_skip = lax.dynamic_slice_in_dim(skip, first_channel, per_device, 0)
    gated_chan, query_chan = (
        lax.all_to_all(gated, "ctx", split_axis=0, concat_axis=1, tiled=True),
        lax.all_to_all(query, "ctx", split_axis=0, concat_axis=1, tiled=True),
    )
    mixed_chan = long_conv(gated_chan, own_residues, own_rates, own_skip)
    output_chan = (query_chan.astype(jnp.float32) * mixed_chan.astype(jnp.float32)).astype(
        jnp.bfloat16
    )
    output = lax.all_to_all(output_chan, "ctx", split_axis=1, concat_axis=0, tiled=True)
    return output


def solution(mesh):
    in_specs = (P(None, "tp", "ctx"), P(None, None, "tp"), P(None, "tp"), P(None, "tp"), P("tp"))
    out_specs = P("tp", "ctx")
    return jax.shard_map(
        on_device, mesh=mesh, in_specs=in_specs, out_specs=out_specs, check_vma=False
    )
```

profile of v0, /device:TPU:0, one launch (start us, length us, event | category | flops | bytes accessed | tf_op | source)
XLA Modules:
  0.0 782.8 jit_solution(15507286830214267869)
XLA Ops:
  7.6 25.3 %multiply_add_fusion.1 = f32[3,1024,2048]{2,1,0:T(8,128)S(1)} fusion(bf16[3,1024,2048]{2,1,0:T(8,128)(2,1)} %param.7, bf16[3,1024,2]{2,1,0:T(8,128)(2,1)S(1)} %copy.116, f32[3,1024]{1,0:T(4,128)S(1)} %get-tuple-element.249, f32[3,1024]{1,0:T(4,128)S(1)} %get-tuple-element.250, f32[3,1024]{1,0:T(4,128)S(1)} %bitcast.246), kind=kLoop, calls=%fused_computation.192 | loop fusion | flops 88080384 | bytes 37797888 | tf_op jit(solution)/shard_map/add | solution.py:102
  60.8 48.8 %all-to-all-done.1 = bf16[32,32,2048]{2,1,0:T(8,128)(2,1)} async-done(((bf16[32,32,2048]{2,1,0:T(8,128)(2,1)}), bf16[32,32,2048]{2,1,0:T(8,128)(2,1)}, u32[]{:S(2)}, u32[]{:S(2)}) %all-to-all-start.1) | async-done | bytes 4194336 | tf_op jit(solution)/shard_map/all_to_all | solution.py:113
  126.6 578.0 %while.12 = (s32[]{:T(128)}, bf16[4,8,65536]{2,1,0:T(8,128)(2,1)}, bf16[4,8,65536]{2,1,0:T(8,128)(2,1)}, f32[4,16,8]{1,2,0:T(8,128)S(1)}, f32[4,16,8]{1,2,0:T(8,128)S(1)}, /*index=5*/f32[4,8]{1,0:T(4,128)S(1)}, s32[]{:T(128)}) while((s32[]{:T(128)}, bf16[4,8,65536]{2,1,0:T(8,128)(2,1)}, bf16[4,8,65536]{2,1,0:T(8,128)(2,1)}, ...), condition=%wide.region_2.3_spmd.clone.clone, body=%wide.region_0.2_spmd.clone.clone.sunk | while | flops 29113286656 | bytes 267392240 | solution.py:91
  136.3 13.8 %fusion.280 = f32[8,128,1024]{2,1,0:T(8,128)S(1)} fusion(f32[1,8,512,128]{3,1,2,0:T(8,128)S(1)} %bitcast.247), kind=kOutput, calls=%fused_computation.47.clone.1 | convolution fusion | flops 3228565504 | bytes 6291456 | tf_op jit(solution)/shard_map/while/body/eval_jaxpr/kh,ghn->gkn/dot_general | solution.py:29
  150.1 14.2 %fusion.279 = f32[8,128,1024]{2,1,0:T(8,128)S(1)} fusion(f32[1,8,512,128]{3,1,2,0:T(8,128)S(1)} %bitcast.248), kind=kOutput, calls=%fused_computation.45.clone.1 | convolution fusion | flops 3229089792 | bytes 6291456 | tf_op jit(solution)/shard_map/while/body/eval_jaxpr/kh,ghn->gkn/dot_general | solution.py:30
  164.3 10.2 %fusion.283 = f32[8,128,1024]{2,1,0:T(8,128)S(1)} fusion(bf16[1,8,512,128]{3,1,2,0:T(8,128)(2,1)S(1)} %dynamic-slice_bitcast_fusion.2), kind=kOutput, calls=%fused_computation.55.clone.1 | convolution fusion | flops 3228565504 | bytes 5242880 | tf_op jit(solution)/shard_map/while/body/eval_jaxpr/kh,ghn->gkn/dot_general | solution.py:29
  174.5 10.6 %fusion.282 = f32[8,128,1024]{2,1,0:T(8,128)S(1)} fusion(bf16[1,8,512,128]{3,1,2,0:T(8,128)(2,1)S(1)} %dynamic-slice_bitcast_fusion.2), kind=kOutput, calls=%fused_computation.51.clone.1 | convolution fusion | flops 3229089792 | bytes 5242880 | tf_op jit(solution)/shard_map/while/body/eval_jaxpr/kh,ghn->gkn/dot_general | solution.py:30
  221.4 9.9 %multiply_add_fusion.3 = (f32[8,1024,128]{2,1,0:T(8,128)}, f32[8,1024,128]{2,1,0:T(8,128)S(1)}) fusion(f32[8,1024,128]{2,1,0:T(8,128)} %convolution_subtract_fusion.6, f32[8,1024,128]{2,1,0:T(8,128)} %convolution_subtract_fusion.7, f32[8,1024,128]{2,1,0:T(8,128)} %convolution_add_fusion.5, f32[8,1024,128]{2,1,0:T(8,128)} %fusion.286, ...), kind=kOutput, calls=%fused_computation.31.clone.1 | convolution fusion | flops 816021504 | bytes 34603008 | tf_op jit(solution)/shard_map/while/body/eval_jaxpr/gkn,nm->gkm/dot_general | solution.py:36
  240.1 11.5 %fusion.289 = f32[8,128,512]{2,1,0:T(8,128)S(1)} fusion(f32[8,1024,128]{1,2,0:T(8,128)S(1)} %convolution_add_fusion.6, f32[8,1024,128]{1,2,0:T(8,128)S(1)} %convolution_subtract_fusion.8, f32[1024,128]{0,1:T(8,128)S(1)} %get-tuple-element.298, f32[1024,128]{0,1:T(8,128)S(1)} %get-tuple-element.299), kind=kOutput, calls=%fused_computation.23.clone.1 | convolution fusion | flops 3232235520 | bytes 11534336 | tf_op jit(solution)/shard_map/while/body/eval_jaxpr/kh,gkn->ghn/dot_general | solution.py:52
  251.6 11.4 %multiply_bitcast_fusion.5 = f32[8,512,128]{1,2,0:T(8,128)S(1)} fusion(f32[8,128,512]{2,1,0:T(8,128)S(1)} %fusion.289, f32[8,1024,128]{1,2,0:T(8,128)S(1)} %convolution_subtract_fusion.8, f32[8,1024,128]{1,2,0:T(8,128)S(1)} %convolution_add_fusion.6, f32[1024,128]{0,1:T(8,128)S(1)} %get-tuple-element.298, f32[1024,128]{0,1:T(8,128)S(1)} %get-tuple-element.299), kind=kOutput, calls=%fused_computation.61.clone.1 | convolution fusion | flops 3232759808 | bytes 13631488 | tf_op jit(solution)/shard_map/while/body/eval_jaxpr/kh,gkn->ghn/dot_general | solution.py:52
  279.4 13.7 %fusion.280 = f32[8,128,1024]{2,1,0:T(8,128)S(1)} fusion(f32[1,8,512,128]{3,1,2,0:T(8,128)S(1)} %bitcast.247), kind=kOutput, calls=%fused_computation.47.clone.1 | convolution fusion | flops 3228565504 | bytes 6291456 | tf_op jit(solution)/shard_map/while/body/eval_jaxpr/kh,ghn->gkn/dot_general | solution.py:29
  293.2 14.3 %fusion.279 = f32[8,128,1024]{2,1,0:T(8,128)S(1)} fusion(f32[1,8,512,128]{3,1,2,0:T(8,128)S(1)} %bitcast.248), kind=kOutput, calls=%fused_computation.45.clone.1 | convolution fusion | flops 3229089792 | bytes 6291456 | tf_op jit(solution)/shard_map/while/body/eval_jaxpr/kh,ghn->gkn/dot_general | solution.py:30
  307.5 10.2 %fusion.283 = f32[8,128,1024]{2,1,0:T(8,128)S(1)} fusion(bf16[1,8,512,128]{3,1,2,0:T(8,128)(2,1)S(1)} %dynamic-slice_bitcast_fusion.2), kind=kOutput, calls=%fused_computation.55.clone.1 | convolution fusion | flops 3228565504 | bytes 5242880 | tf_op jit(solution)/shard_map/while/body/eval_jaxpr/kh,ghn->gkn/dot_general | solution.py:29
  317.7 10.5 %fusion.282 = f32[8,128,1024]{2,1,0:T(8,128)S(1)} fusion(bf16[1,8,512,128]{3,1,2,0:T(8,128)(2,1)S(1)} %dynamic-slice_bitcast_fusion.2), kind=kOutput, calls=%fused_computation.51.clone.1 | convolution fusion | flops 3229089792 | bytes 5242880 | tf_op jit(solution)/shard_map/while/body/eval_jaxpr/kh,ghn->gkn/dot_general | solution.py:30
  364.5 9.7 %multiply_add_fusion.3 = (f32[8,1024,128]{2,1,0:T(8,128)}, f32[8,1024,128]{2,1,0:T(8,128)S(1)}) fusion(f32[8,1024,128]{2,1,0:T(8,128)} %convolution_subtract_fusion.6, f32[8,1024,128]{2,1,0:T(8,128)} %convolution_subtract_fusion.7, f32[8,1024,128]{2,1,0:T(8,128)} %convolution_add_fusion.5, f32[8,1024,128]{2,1,0:T(8,128)} %fusion.286, ...), kind=kOutput, calls=%fused_computation.31.clone.1 | convolution fusion | flops 816021504 | bytes 34603008 | tf_op jit(solution)/shard_map/while/body/eval_jaxpr/gkn,nm->gkm/dot_general | solution.py:36
  383.0 11.5 %fusion.289 = f32[8,128,512]{2,1,0:T(8,128)S(1)} fusion(f32[8,1024,128]{1,2,0:T(8,128)S(1)} %convolution_add_fusion.6, f32[8,1024,128]{1,2,0:T(8,128)S(1)} %convolution_subtract_fusion.8, f32[1024,128]{0,1:T(8,128)S(1)} %get-tuple-element.298, f32[1024,128]{0,1:T(8,128)S(1)} %get-tuple-element.299), kind=kOutput, calls=%fused_computation.23.clone.1 | convolution fusion | flops 3232235520 | bytes 11534336 | tf_op jit(solution)/shard_map/while/body/eval_jaxpr/kh,gkn->ghn/dot_general | solution.py:52
  394.6 11.6 %multiply_bitcast_fusion.5 = f32[8,512,128]{1,2,0:T(8,128)S(1)} fusion(f32[8,128,512]{2,1,0:T(8,128)S(1)} %fusion.289, f32[8,1024,128]{1,2,0:T(8,128)S(1)} %convolution_subtract_fusion.8, f32[8,1024,128]{1,2,0:T(8,128)S(1)} %convolution_add_fusion.6, f32[1024,128]{0,1:T(8,128)S(1)} %get-tuple-element.298, f32[1024,128]{0,1:T(8,128)S(1)} %get-tuple-element.299), kind=kOutput, calls=%fused_computation.61.clone.1 | convolution fusion | flops 3232759808 | bytes 13631488 | tf_op jit(solution)/shard_map/while/body/eval_jaxpr/kh,gkn->ghn/dot_general | solution.py:52
  422.3 13.8 %fusion.280 = f32[8,128,1024]{2,1,0:T(8,128)S(1)} fusion(f32[1,8,512,128]{3,1,2,0:T(8,128)S(1)} %bitcast.247), kind=kOutput, calls=%fused_computation.47.clone.1 | convolution fusion | flops 3228565504 | bytes 6291456 | tf_op jit(solution)/shard_map/while/body/eval_jaxpr/kh,ghn->gkn/dot_general | solution.py:29
  436.1 14.2 %fusion.279 = f32[8,128,1024]{2,1,0:T(8,128)S(1)} fusion(f32[1,8,512,128]{3,1,2,0:T(8,128)S(1)} %bitcast.248), kind=kOutput, calls=%fused_computation.45.clone.1 | convolution fusion | flops 3229089792 | bytes 6291456 | tf_op jit(solution)/shard_map/while/body/eval_jaxpr/kh,ghn->gkn/dot_general | solution.py:30
  450.4 10.2 %fusion.283 = f32[8,128,1024]{2,1,0:T(8,128)S(1)} fusion(bf16[1,8,512,128]{3,1,2,0:T(8,128)(2,1)S(1)} %dynamic-slice_bitcast_fusion.2), kind=kOutput, calls=%fused_computation.55.clone.1 | convolution fusion | flops 3228565504 | bytes 5242880 | tf_op jit(solution)/shard_map/while/body/eval_jaxpr/kh,ghn->gkn/dot_general | solution.py:29
  460.6 10.6 %fusion.282 = f32[8,128,1024]{2,1,0:T(8,128)S(1)} fusion(bf16[1,8,512,128]{3,1,2,0:T(8,128)(2,1)S(1)} %dynamic-slice_bitcast_fusion.2), kind=kOutput, calls=%fused_computation.51.clone.1 | convolution fusion | flops 3229089792 | bytes 5242880 | tf_op jit(solution)/shard_map/while/body/eval_jaxpr/kh,ghn->gkn/dot_general | solution.py:30
  507.4 9.9 %multiply_add_fusion.3 = (f32[8,1024,128]{2,1,0:T(8,128)}, f32[8,1024,128]{2,1,0:T(8,128)S(1)}) fusion(f32[8,1024,128]{2,1,0:T(8,128)} %convolution_subtract_fusion.6, f32[8,1024,128]{2,1,0:T(8,128)} %convolution_subtract_fusion.7, f32[8,1024,128]{2,1,0:T(8,128)} %convolution_add_fusion.5, f32[8,1024,128]{2,1,0:T(8,128)} %fusion.286, ...), kind=kOutput, calls=%fused_computation.31.clone.1 | convolution fusion | flops 816021504 | bytes 34603008 | tf_op jit(solution)/shard_map/while/body/eval_jaxpr/gkn,nm->gkm/dot_general | solution.py:36
  526.2 11.5 %fusion.289 = f32[8,128,512]{2,1,0:T(8,128)S(1)} fusion(f32[8,1024,128]{1,2,0:T(8,128)S(1)} %convolution_add_fusion.6, f32[8,1024,128]{1,2,0:T(8,128)S(1)} %convolution_subtract_fusion.8, f32[1024,128]{0,1:T(8,128)S(1)} %get-tuple-element.298, f32[1024,128]{0,1:T(8,128)S(1)} %get-tuple-element.299), kind=kOutput, calls=%fused_computation.23.clone.1 | convolution fusion | flops 3232235520 | bytes 11534336 | tf_op jit(solution)/shard_map/while/body/eval_jaxpr/kh,gkn->ghn/dot_general | solution.py:52
  537.7 11.4 %multiply_bitcast_fusion.5 = f32[8,512,128]{1,2,0:T(8,128)S(1)} fusion(f32[8,128,512]{2,1,0:T(8,128)S(1)} %fusion.289, f32[8,1024,128]{1,2,0:T(8,128)S(1)} %convolution_subtract_fusion.8, f32[8,1024,128]{1,2,0:T(8,128)S(1)} %convolution_add_fusion.6, f32[1024,128]{0,1:T(8,128)S(1)} %get-tuple-element.298, f32[1024,128]{0,1:T(8,128)S(1)} %get-tuple-element.299), kind=kOutput, calls=%fused_computation.61.clone.1 | convolution fusion | flops 3232759808 | bytes 13631488 | tf_op jit(solution)/shard_map/while/body/eval_jaxpr/kh,gkn->ghn/dot_general | solution.py:52
  565.4 13.7 %fusion.280 = f32[8,128,1024]{2,1,0:T(8,128)S(1)} fusion(f32[1,8,512,128]{3,1,2,0:T(8,128)S(1)} %bitcast.247), kind=kOutput, calls=%fused_computation.47.clone.1 | convolution fusion | flops 3228565504 | bytes 6291456 | tf_op jit(solution)/shard_map/while/body/eval_jaxpr/kh,ghn->gkn/dot_general | solution.py:29
  579.2 14.3 %fusion.279 = f32[8,128,1024]{2,1,0:T(8,128)S(1)} fusion(f32[1,8,512,128]{3,1,2,0:T(8,128)S(1)} %bitcast.248), kind=kOutput, calls=%fused_computation.45.clone.1 | convolution fusion | flops 3229089792 | bytes 6291456 | tf_op jit(solution)/shard_map/while/body/eval_jaxpr/kh,ghn->gkn/dot_general | solution.py:30
  593.5 10.2 %fusion.283 = f32[8,128,1024]{2,1,0:T(8,128)S(1)} fusion(bf16[1,8,512,128]{3,1,2,0:T(8,128)(2,1)S(1)} %dynamic-slice_bitcast_fusion.2), kind=kOutput, calls=%fused_computation.55.clone.1 | convolution fusion | flops 3228565504 | bytes 5242880 | tf_op jit(solution)/shard_map/while/body/eval_jaxpr/kh,ghn->gkn/dot_general | solution.py:29
  603.7 10.5 %fusion.282 = f32[8,128,1024]{2,1,0:T(8,128)S(1)} fusion(bf16[1,8,512,128]{3,1,2,0:T(8,128)(2,1)S(1)} %dynamic-slice_bitcast_fusion.2), kind=kOutput, calls=%fused_computation.51.clone.1 | convolution fusion | flops 3229089792 | bytes 5242880 | tf_op jit(solution)/shard_map/while/body/eval_jaxpr/kh,ghn->gkn/dot_general | solution.py:30
  650.5 9.7 %multiply_add_fusion.3 = (f32[8,1024,128]{2,1,0:T(8,128)}, f32[8,1024,128]{2,1,0:T(8,128)S(1)}) fusion(f32[8,1024,128]{2,1,0:T(8,128)} %convolution_subtract_fusion.6, f32[8,1024,128]{2,1,0:T(8,128)} %convolution_subtract_fusion.7, f32[8,1024,128]{2,1,0:T(8,128)} %convolution_add_fusion.5, f32[8,1024,128]{2,1,0:T(8,128)} %fusion.286, ...), kind=kOutput, calls=%fused_computation.31.clone.1 | convolution fusion | flops 816021504 | bytes 34603008 | tf_op jit(solution)/shard_map/while/body/eval_jaxpr/gkn,nm->gkm/dot_general | solution.py:36
  669.1 11.5 %fusion.289 = f32[8,128,512]{2,1,0:T(8,128)S(1)} fusion(f32[8,1024,128]{1,2,0:T(8,128)S(1)} %convolution_add_fusion.6, f32[8,1024,128]{1,2,0:T(8,128)S(1)} %convolution_subtract_fusion.8, f32[1024,128]{0,1:T(8,128)S(1)} %get-tuple-element.298, f32[1024,128]{0,1:T(8,128)S(1)} %get-tuple-element.299), kind=kOutput, calls=%fused_computation.23.clone.1 | convolution fusion | flops 3232235520 | bytes 11534336 | tf_op jit(solution)/shard_map/while/body/eval_jaxpr/kh,gkn->ghn/dot_general | solution.py:52
  680.6 11.6 %multiply_bitcast_fusion.5 = f32[8,512,128]{1,2,0:T(8,128)S(1)} fusion(f32[8,128,512]{2,1,0:T(8,128)S(1)} %fusion.289, f32[8,1024,128]{1,2,0:T(8,128)S(1)} %convolution_subtract_fusion.8, f32[8,1024,128]{1,2,0:T(8,128)S(1)} %convolution_add_fusion.6, f32[1024,128]{0,1:T(8,128)S(1)} %get-tuple-element.298, f32[1024,128]{0,1:T(8,128)S(1)} %get-tuple-element.299), kind=kOutput, calls=%fused_computation.61.clone.1 | convolution fusion | flops 3232759808 | bytes 13631488 | tf_op jit(solution)/shard_map/while/body/eval_jaxpr/kh,gkn->ghn/dot_general | solution.py:52
  722.0 58.7 %all_to_all.39 = bf16[32,32,2048]{2,0,1:T(8,128)(2,1)S(1)} all-to-all(bf16[32,32,2048]{2,0,1:T(8,128)(2,1)S(1)} %fusion.190), channel_id=1, replica_groups=mesh['ctx'=32,'tp'=4] {'ctx'}, dimensions={1} | all-to-all | bytes 8388608 | tf_op jit(solution)/shard_map/all_to_all | solution.py:120
  (118 shorter events, 315.9 us)
Async XLA Ops:
  1.8 5.3 collective-permute-start
  32.8 8.3 %copy-start.1 = (f32[3,1024,2048]{2,1,0:T(8,128)}, f32[3,1024,2048]{2,1,0:T(8,128)S(1)}, u32[]{:S(2)}) copy-start(f32[3,1024,2048]{2,1,0:T(8,128)S(1)} %multiply_add_fusion.1) | copy-start | bytes 75497472
  43.8 65.8 %all-to-all-start.1 = ((bf16[32,32,2048]{2,1,0:T(8,128)(2,1)}), bf16[32,32,2048]{2,1,0:T(8,128)(2,1)}, u32[]{:S(2)}, u32[]{:S(2)}) async-start(bf16[32,32,2048]{2,1,0:T(8,128)(2,1)} %bitcast.240), calls=%async_computation.1 | async-start | bytes 8388608 | tf_op jit(solution)/shard_map/all_to_all | solution.py:113
  109.6 602.9 %all-to-all-start = ((bf16[32,32,2048]{2,1,0:T(8,128)(2,1)}), bf16[32,32,2048]{2,1,0:T(8,128)(2,1)}, u32[]{:S(2)}, u32[]{:S(2)}) async-start(bf16[32,32,2048]{2,1,0:T(8,128)(2,1)} %bitcast.241), calls=%async_computation | async-start | bytes 8388608 | tf_op jit(solution)/shard_map/all_to_all | solution.py:114
  231.3 2.2 copy-start
  374.2 2.2 copy-start
  517.4 2.2 copy-start
  660.3 2.2 copy-start
where the time goes:
time: 791 us; the launch traced here: 783 us
  matrix products  506 us (64%)
  other arithmetic  80.3 us (10%)
  local copies, waits for them, and re-layouts  62.5 us (8%)
  blocking collectives  58.7 us (7%)
  waiting for transfers between devices  49.2 us (6%)
  starting transfers between devices  18 us (2%)
    dot_general x8, matrix products, forward_spectrum(): part_im = jnp.einsum('kh,ghn->gkn', first_im, signal, precision=PRECISE)  99.2 us
    dot_general x8, matrix products, forward_spectrum(): part_re = jnp.einsum('kh,ghn->gkn', first_re, signal, precision=PRECISE)  95.9 us
    dot_general x8, matrix products, forward_spectrum(): jnp.einsum('gkn,nm->gkm', turned_im, second_re, precision=PRECISE)  62.5 us
    all_to_all x1, blocking collectives, on_device(): lax.all_to_all(output_chan, 'ctx', split_axis=1, concat_axis=0, tiled=True)  58.7 us
    all_to_all x1, waiting for transfers between devices, on_device(): lax.all_to_all(gated, 'ctx', split_axis=0, concat_axis=1, tiled=True)  48.8 us
    dot_general x8, matrix products, forward_spectrum(): jnp.einsum('gkn,nm->gkm', turned_im, second_im, precision=PRECISE)  48.4 us
    dot_general x4, matrix products, inverse_first_half(): jnp.einsum('kh,gkn->ghn', first_im, turned_im, precision=PRECISE)  46 us
    dot_general x4, matrix products, inverse_first_half(): jnp.einsum('kh,gkn->ghn', first_re, turned_re, precision=PRECISE)  45.9 us
  transfers between devices with their start and end apart: 3, of which 2 were waited for; matrix products, arithmetic and copies ran while one was open for 76% of the time, Pallas kernels for 0%

commit v1 on v0

v1 whole, which is shorter than its diff:
```python
import jax
import jax.numpy as jnp
from jax import lax
from jax.experimental import pallas as pl
from jax.experimental.pallas import tpu as pltpu
from jax.sharding import PartitionSpec as P

F32 = jnp.float32
BF16 = jnp.bfloat16
WIDE = F32
SHORT = 3
MODES = 16
GROUP = 8
STEP = 16
LANES = 128
VMEM = 52 * 1024 * 1024
SMALL = 16 * 1024 * 1024


def cat(parts, axis=0):
    return jnp.concatenate(parts, axis=axis)


def iota(shape, dim):
    return lax.broadcasted_iota(jnp.int32, shape, dim)


def split(x):
    high = x.astype(BF16)
    return high, (x - high.astype(F32)).astype(BF16)


def filtered(load, rim, taps, count):
    lane = iota((16, LANES), 1)
    first, second = lane < 1, lane < 2
    before1, before2 = pltpu.roll(rim, 1, 1), pltpu.roll(rim, 2, 1)
    for k in range(count):
        here = load(k)
        turned1, turned2 = pltpu.roll(here, 1, 1), pltpu.roll(here, 2, 1)
        back1 = jnp.where(first, before1, turned1)
        back2 = jnp.where(second, before2, turned2)
        yield taps[0] * here.astype(F32) + taps[1] * back1.astype(F32) + taps[2] * back2.astype(F32)
        before1, before2 = turned1, turned2


def swap_blocks(tiles):
    lane = iota(tiles[0].shape, 1) // STEP
    tiles = [pltpu.roll(x, STEP * c, 1) if c else x for c, x in enumerate(tiles)]
    for d in (4, 2, 1):
        keep = (lane & d) == 0
        tiles = [jnp.where(keep, tiles[j], tiles[(j + d) % 8]) for j in range(8)]
    tiles = [tiles[-j % 8] for j in range(8)]
    return [pltpu.roll(x, LANES - STEP * j, 1) if j else x for j, x in enumerate(tiles)]


def spread(base):
    lane = iota(base.shape, 1) // STEP
    return cat([jnp.where(lane == c, base, jnp.zeros_like(base)) for c in range(GROUP)], 0)


def decay_in(rate):
    row = iota((STEP, LANES), 0).astype(F32)
    high, low = split(jnp.exp(rate * (row - float(STEP))))
    return cat([spread(high), spread(low)], 0)


def table_kernel(residues, rates, skips, tables):
    lane = iota((STEP, LANES), 1)
    place = (lane % STEP).astype(F32)
    row = iota((STEP, LANES), 0)
    after = (lane % STEP) >= row
    same = (lane % STEP) == row

    def tile(i, _):
        cols = pl.ds(pl.multiple_of(i * LANES, LANES), LANES)
        rate16, residue16 = rates[:, cols], residues[:, cols]
        weight16 = residue16 * jnp.sqrt(2.0 * rate16)
        skip16 = jnp.broadcast_to(skips[:, cols], (STEP, LANES))
        for j in range(LANES // GROUP):
            at = lane // STEP + GROUP * j
            rate = jnp.take_along_axis(rate16, at, axis=1)
            weight = jnp.take_along_axis(weight16, at, axis=1)
            skip = jnp.take_along_axis(skip16, at, axis=1)
            out = weight * jnp.exp(-rate * place)
            taps = jnp.broadcast_to(jnp.sum(out, axis=0, keepdims=True), (STEP, LANES))
            near = pltpu.roll(taps, 0, 1, stride=1, stride_axis=0)
            near = jnp.where(after, near, 0.0) + jnp.where(same, skip, 0.0)
            g = i * (LANES // GROUP) + j
            tables[g] = cat([*split(out), *split(near)], 0)
        return 0

    lax.fori_loop(0, rates.shape[1] // LANES, tile, 0)


def gate_kernel(streams, rims, taps, rates, gated, sums, state, xs, zs):
    tiles = streams.shape[2] // LANES
    pairs = streams.shape[1] // 16
    segment = streams.shape[2] // 8
    unroll = xs.shape[0]
    left = 7.0 - iota((8, LANES), 0).astype(F32)

    def step(i, _):
        for u in range(unroll):
            rows = pl.ds(pl.multiple_of((i * unroll + u) * 16, 16), 16)
            sides = []
            for s in (0, 1):
                tap = [
                    jnp.broadcast_to(taps[rows, pl.ds(3 * (s + 1) + j, 1)], (16, LANES)) for j in range(SHORT)
                ]
                load = lambda k, s=s, rows=rows: streams[s, rows, pl.ds(k * LANES, LANES)].astype(WIDE)
                sides.append(filtered(load, rims[s, rows, :].astype(WIDE), tap, tiles))
            for k, (a, b) in enumerate(zip(*sides)):
                xs[u, k % 2, pl.ds(k // 2 * 16, 16), :] = a * b
        for v in range(2 * unroll):
            g = i * 2 * unroll + v
            u, half = v // 2, v % 2
            lined = [
                cat([xs[u, odd, pl.ds(8 * half + c, 8, stride=16), :] for odd in (0, 1)], 0).astype(BF16)
                for c in range(GROUP)
            ]
            gated[g] = cat(swap_blocks(lined), 0)
        for v in range(2 * unroll):
            g = i * 2 * unroll + v
            x = gated[g]
            zs[v] = jnp.dot(cat([x, x], 1), decay_in(rates[pl.ds(g, 1), :]), preferred_element_type=F32)
        for v in range(2 * unroll):
            g = i * 2 * unroll + v
            rate = rates[pl.ds(g, 1), :]
            over = jnp.exp(-float(STEP) * rate)
            held = zs[v, 0:8, :]
            for k in range(1, 16):
                at = 16 * (k % 8) + 8 * (k // 8)
                held = held * over + zs[v, at : at + 8, :]
            sums[g] = held
            state[pl.ds(g, 1), :] = jnp.sum(
                held * jnp.exp(-float(segment) * rate * left), axis=0, keepdims=True
            )
        return 0

    lax.fori_loop(0, pairs // unroll, step, 0)


def query_kernel(streams, rims, taps, query):
    tiles = streams.shape[2] // LANES

    def pair(i, _):
        rows = pl.ds(pl.multiple_of(i * 16, 16), 16)
        tap = [jnp.broadcast_to(taps[rows, pl.ds(j, 1)], (16, LANES)) for j in range(SHORT)]
        load = lambda k: streams[0, rows, pl.ds(k * LANES, LANES)].astype(WIDE)
        for k, tile in enumerate(filtered(load, rims[0, rows, :].astype(WIDE), tap, tiles)):
            query[rows, pl.ds(k * LANES, LANES)] = tile.astype(BF16)
        return 0

    lax.fori_loop(0, streams.shape[1] // 16, pair, 0, unroll=2)


def mix_kernel(gated, sums, query, rates, tables, before, out, ys, zs):
    tiles = query.shape[1] // LANES
    pairs = query.shape[0] // 16
    segment = query.shape[1] // 8
    unroll = ys.shape[0]
    row = iota((8, LANES), 0)

    def step(i, _):
        for v in range(2 * unroll):
            g = i * 2 * unroll + v
            x = gated[g]
            zs[v] = jnp.dot(cat([x, x], 1), decay_in(rates[pl.ds(g, 1), :]), preferred_element_type=F32)
        for v in range(2 * unroll):
            g = i * 2 * unroll + v
            rate = rates[pl.ds(g, 1), :]
            over = jnp.exp(-float(STEP) * rate)
            first = jnp.broadcast_to(before[pl.ds(g, 1), :], (8, LANES))
            held = jnp.where(row == 0, first, pltpu.roll(sums[g], 1, 0))
            for d in (1, 2, 4):
                earlier = jnp.where(row < d, 0.0, pltpu.roll(held, d, 0))
                held = held + jnp.exp(-float(segment * d) * rate) * earlier
            for k in range(16):
                at = 16 * (k % 8) + 8 * (k // 8)
                entering = zs[v, at : at + 8, :]
                zs[v, at : at + 8, :] = held
                held = held * over + entering
        for v in range(2 * unroll):
            g = i * 2 * unroll + v
            x = gated[g]
            high, low = split(zs[v])
            base = tables[g]
            far_high, far_low, near_high, near_low = [spread(base[16 * n : 16 * n + 16]) for n in range(4)]
            zs[v] = jnp.dot(
                cat([high, high, low, x, x], 1),
                cat([far_high, far_low, far_high, near_high, near_low], 0),
                preferred_element_type=F32,
            )
        for v in range(2 * unroll):
            u, half = v // 2, v % 2
            lined = swap_blocks([zs[v, 16 * b : 16 * b + 16, :].astype(BF16) for b in range(8)])
            for c in range(GROUP):
                wide = lined[c].astype(F32)
                for odd in (0, 1):
                    ys[u, odd, pl.ds(8 * half + c, 8, stride=16), :] = wide[8 * odd : 8 * odd + 8]
        for u in range(unroll):
            rows = pl.ds(pl.multiple_of((i * unroll + u) * 16, 16), 16)
            for k in range(tiles):
                mixed = ys[u, k % 2, pl.ds(k // 2 * 16, 16), :].astype(BF16)
                cols = pl.ds(k * LANES, LANES)
                out[rows, cols] = query[rows, cols] * mixed
        return 0

    lax.fori_loop(0, pairs // unroll, step, 0)


def make_tables(residues, rates, skip):
    channels = rates.shape[1]
    groups = channels // GROUP
    return pl.pallas_call(
        table_kernel,
        out_shape=jax.ShapeDtypeStruct((groups, 4 * STEP, LANES), BF16),
        compiler_params=pltpu.CompilerParams(vmem_limit_bytes=SMALL),
        name="tables",
    )(residues, rates, skip[None, :])


def make_query(streams, rims, taps, block):
    channels, length = streams.shape[1:]
    return pl.pallas_call(
        query_kernel,
        grid=(channels // block,),
        in_specs=[
            pl.BlockSpec((1, block, length), lambda i: (0, i, 0)),
            pl.BlockSpec((1, block, LANES), lambda i: (0, i, 0)),
            pl.BlockSpec((block, 9), lambda i: (i, 0)),
        ],
        out_specs=pl.BlockSpec((block, length), lambda i: (i, 0)),
        out_shape=jax.ShapeDtypeStruct((channels, length), BF16),
        compiler_params=pltpu.CompilerParams(vmem_limit_bytes=VMEM),
        cost_estimate=pl.CostEstimate(flops=channels * length * 1024, bytes_accessed=4 * channels * length, transcendentals=0),
        name="query",
    )(streams, rims, taps)


def gate(streams, rims, taps, rates, block, unroll=8):
    channels, length = streams.shape[1:]
    groups = channels // GROUP
    rows = length // STEP
    bg = block // GROUP
    return pl.pallas_call(
        gate_kernel,
        grid=(channels // block,),
        in_specs=[
            pl.BlockSpec((pl.Element(2), pl.Element(block), pl.Element(length)), lambda i: (1, i * block, 0)),
            pl.BlockSpec((pl.Element(2), pl.Element(block), pl.Element(LANES)), lambda i: (1, i * block, 0)),
            pl.BlockSpec((block, 9), lambda i: (i, 0)),
            pl.BlockSpec((bg, LANES), lambda i: (i, 0)),
        ],
        out_specs=[
            pl.BlockSpec((bg, rows, LANES), lambda i: (i, 0, 0)),
            pl.BlockSpec((bg, 8, LANES), lambda i: (i, 0, 0)),
            pl.BlockSpec((bg, LANES), lambda i: (i, 0)),
        ],
        out_shape=[
            jax.ShapeDtypeStruct((groups, rows, LANES), BF16),
            jax.ShapeDtypeStruct((groups, 8, LANES), F32),
            jax.ShapeDtypeStruct((groups, LANES), F32),
        ],
        scratch_shapes=[pltpu.VMEM((unroll, 2, rows, LANES), F32), pltpu.VMEM((2 * unroll, rows, LANES), F32)],
        compiler_params=pltpu.CompilerParams(vmem_limit_bytes=VMEM),
        name="gate",
    )(streams, rims, taps, rates)


def mix(gated, sums, query, rates, tables, before, block, unroll=8):
    channels, length = query.shape
    rows = length // STEP
    bg = block // GROUP
    return pl.pallas_call(
        mix_kernel,
        grid=(channels // block,),
        in_specs=[
            pl.BlockSpec((bg, rows, LANES), lambda i: (i, 0, 0)),
            pl.BlockSpec((bg, 8, LANES), lambda i: (i, 0, 0)),
            pl.BlockSpec((block, length), lambda i: (i, 0)),
            pl.BlockSpec((bg, LANES), lambda i: (i, 0)),
            pl.BlockSpec((bg, 4 * STEP, LANES), lambda i: (i, 0, 0)),
            pl.BlockSpec((bg, LANES), lambda i: (i, 0)),
        ],
        out_specs=pl.BlockSpec((block, length), lambda i: (i, 0)),
        out_shape=jax.ShapeDtypeStruct((channels, length), BF16),
        scratch_shapes=[pltpu.VMEM((unroll, 2, rows, LANES), F32), pltpu.VMEM((2 * unroll, rows, LANES), F32)],
        compiler_params=pltpu.CompilerParams(vmem_limit_bytes=VMEM),
        name="mix",
    )(gated, sums, query, rates, tables, before)


def states_before(state, rates, length):
    axis = "ctx"
    index = lax.axis_index(axis)
    devices = lax.axis_size(axis)

    def decay(times):
        return jnp.exp(-float(length) * rates * jnp.asarray(times, F32))

    before = jnp.zeros_like(state)
    total = state
    span = 1
    for size in (2, 4, 4):
        place = (index // span) % size

        def moved(by):
            pairs = []
            for i in range(devices):
                at = (i // span) % size
                pairs.append((i, i + ((at + by) % size - at) * span))
            return lax.ppermute(total, axis, pairs)

        others = [moved(by) for by in range(1, size)]
        prefix = jnp.zeros_like(state)
        whole = decay(span * (size - 1 - place)) * total
        for by, other in enumerate(others, 1):
            at = (place - by) % size
            valid = by <= place
            prefix = prefix + jnp.where(valid, decay(span * jnp.where(valid, by - 1, 0)) * other, 0.0)
            whole = whole + decay(span * (size - 1 - at)) * other
        before = before + decay(index % span) * prefix
        total = whole
        span *= size
    return before


def on_device(streams, short_filters, residues, rates, skip):
    channels, length = streams.shape[1:]
    groups = channels // GROUP

    def by_group(x):
        return x.T.reshape(groups, GROUP * MODES)

    devices = lax.axis_size("ctx")
    edge = streams[:, :, length - (SHORT - 1) :]
    rims = lax.ppermute(edge, "ctx", [(i, i + 1) for i in range(devices - 1)])
    rims = jnp.pad(rims, ((0, 0), (0, 0), (LANES - (SHORT - 1), 0)))
    taps = short_filters.reshape(9, channels).T
    rate = by_group(rates)
    tables = make_tables(residues, rates, skip)
    gated, sums, state = gate(streams, rims, taps, rate, 128)
    query = make_query(streams, rims, taps, 128)
    before = states_before(state, rate, length)
    return mix(gated, sums, query, rate, tables, before, 128)


def solution(mesh):
    in_specs = (P(None, "tp", "ctx"), P(None, None, "tp"), P(None, "tp"), P(None, "tp"), P("tp"))
    out_specs = P("tp", "ctx")
    return jax.shard_map(
        on_device, mesh=mesh, in_specs=in_specs, out_specs=out_specs, check_vma=False
    )
```

time: 791 us -> 69 us (0.09)
  matrix products: 506 us -> 0 us
  other arithmetic: 80.3 us -> 0.19 us
  blocking collectives: 58.7 us -> 0 us
  local copies, waits for them, and re-layouts: 62.5 us -> 6.08 us
  waiting for transfers between devices: 49.2 us -> 3.6 us
  Pallas kernels: 0 us -> 43.4 us
    dot_general x72 -> x0, matrix products: 506 us -> none  [the longest x8 99.2 us: forward_spectrum(): part_im = jnp.einsum('kh,ghn->gkn', first_im, signal, precision=PRECISE)]
    all_to_all x1 -> x0, blocking collectives: 58.7 us -> none  [on_device(): lax.all_to_all(output_chan, 'ctx', split_axis=1, concat_axis=0, tiled=True)]
    all_to_all x2 -> x0, waiting for transfers between devices: 48.8 us -> none  [the longest x1 48.8 us: on_device(): lax.all_to_all(gated, 'ctx', split_axis=0, concat_axis=1, tiled=True)]
    pallas_call x0 -> x4, Pallas kernels: none -> 43.4 us  [the longest x1 17 us: gate(): pl.pallas_call(gate_kernel, grid=(channels // block,), in_specs=[pl.Block...]
    add x1 -> x3, other arithmetic: 25.3 us -> 0.19 us  [the longest x1 0.11 us: states_before(): before = before + decay(index % span) * prefix]
    reduce_sum x4 -> x0, other arithmetic: 24.6 us -> none  [one_block(): jnp.sum((residue_block * jnp.sqrt(2.0 * rate_block))[:, :, None] * jnp.ex...]
    unnamed x7 -> x9, local copies, waits for them, and re-layouts: 18.6 us -> 1.68 us
    all_to_all x2 -> x0, starting transfers between devices: 14 us -> none  [the longest x1 9.18 us: on_device(): lax.all_to_all(gated, 'ctx', split_axis=0, concat_axis=1, tiled=True)]
  transfers between devices with their start and end apart: 3 -> 8, of which waited for: 2 -> 2; matrix products, arithmetic and copies ran while one was open for 76% -> 3% of each run, Pallas kernels for 0% -> 17%
where the time goes in v1:
time: 69 us; the launch traced here: 68.2 us
  Pallas kernels  43.4 us (63%)
  starting transfers between devices  14.8 us (21%)
  local copies, waits for them, and re-layouts  6.08 us (9%)
  waiting for transfers between devices  3.6 us (5%)
    pallas_call x1, Pallas kernels, gate(): pl.pallas_call(gate_kernel, grid=(channels // block,), in_specs=[pl.Block...  17 us
    pallas_call x1, Pallas kernels, mix(): pl.pallas_call(mix_kernel, grid=(channels // block,), in_specs=[pl.BlockS...  14.4 us
    ppermute x7, starting transfers between devices, moved(): return lax.ppermute(total, axis, pairs)  10.9 us
    pallas_call x1, Pallas kernels, make_query(): pl.pallas_call(query_kernel, grid=(channels // block,), in_specs=[pl.Bloc...  9.18 us
    ppermute x1, starting transfers between devices, on_device(): rims = lax.ppermute(edge, 'ctx', [(i, i + 1) for i in range(devices - 1)])  3.9 us
    ppermute x7, waiting for transfers between devices, moved(): return lax.ppermute(total, axis, pairs)  3.59 us
    pallas_call x1, Pallas kernels, make_tables(): pl.pallas_call(table_kernel, out_shape=jax.ShapeDtypeStruct((groups, 4 *...  2.69 us
    unnamed x9, local copies, waits for them, and re-layouts  1.68 us
  transfers between devices with their start and end apart: 8, of which 2 were waited for; matrix products, arithmetic and copies ran while one was open for 3% of the time, Pallas kernels for 17%

profile of v1, /device:TPU:0, one launch (start us, length us, event | category | flops | bytes accessed | tf_op | source)
XLA Modules:
  0.0 68.2 jit_solution(9497338851296365804)
XLA Ops:
  0.0 1.4 %slice.3 = bf16[3,1024,2]{2,1,0:T(8,128)(2,1)S(1)} slice(bf16[3,1024,2048]{2,1,0:T(8,128)(2,1)} %streams.3), slice={[0:3], [0:1024], [2046:2048]} | slice | bytes 24576 | tf_op jit(solution)/shard_map/slice | solution.py:337
  1.4 0.3 copy.14
  1.7 3.9 %collective-permute-start = (bf16[3,1024,2]{1,2,0:T(2,128)(2,1)S(1)}, bf16[3,1024,2]{1,2,0:T(2,128)(2,1)S(1)}, u32[]{:S(2)}, u32[]{:S(2)}) collective-permute-start(bf16[3,1024,2]{1,2,0:T(2,128)(2,1)S(1)} %copy.14), channel_id=1, source_target_pairs={{0,4},{4,8},{8,12},{12,16},{16,20},{20,24},{24,28},{28,32},{32,36}... | collective-permute-start | bytes 36872 | tf_op jit(solution)/shard_map/ppermute | solution.py:338
  5.6 0.8 %reshape.6 = f32[9,1024]{1,0:T(8,128)S(1)} reshape(f32[3,3,1024]{2,1,0:T(4,128)} %param.6) | data formatting | bytes 73728 | tf_op jit(solution)/shard_map/reshape | solution.py:340
  6.4 0.2 copy.12
  6.7 1.0 %copy.13 = f32[1024,16]{1,0:T(8,128)S(1)} copy(f32[1024,16]{0,1:T(8,128)} %bitcast.5) | data formatting | bytes 131072 | tf_op jit(solution)/shard_map/transpose | solution.py:334
  7.7 0.2 reshape.7.rates
  7.9 0.0 collective-permute-done
  7.9 0.4 copy.11
  8.3 0.3 pad.4.rims
  8.7 0.0 copy-start.1
  8.7 0.0 copy-start.2
  8.7 0.0 copy-start.3
  8.7 17.0 %gate.1 = (bf16[128,128,128]{2,1,0:T(8,128)(2,1)}, f32[128,8,128]{2,1,0:T(8,128)S(1)}, f32[128,128]{1,0:T(8,128)S(1)}) custom-call(bf16[3,1024,2048]{2,1,0:T(8,128)(2,1)} %streams.3, bf16[3,1024,128]{2,1,0:T(8,128)(2,1)S(1)} %pad.4.rims, f32[1024,9]{1,0:T(8,128)S(1)} %bitcast.3, f32[128,128]{1,0:T(8,128)S(1)} %reshape.7.rates), custom_call_target="tpu_custom_call" | custom-call | tf_op jit(solution)/shard_map/gate/pallas_call | solution.py:246
  25.7 1.4 %collective-permute-start.1 = (f32[128,128]{1,0:T(8,128)S(1)}, f32[128,128]{1,0:T(8,128)S(1)}, u32[]{:S(2)}, u32[]{:S(2)}) collective-permute-start(f32[128,128]{1,0:T(8,128)S(1)} %get-tuple-element.10), channel_id=1, source_target_pairs={{0,4},{4,0},{8,12},{12,8},{16,20},{20,16},{24,28},{28,24},{32,36},... | collective-permute-start | bytes 196616 | tf_op jit(solution)/shard_map/ppermute | solution.py:313
  27.1 2.9 %collective-permute-done.1 = f32[128,128]{1,0:T(8,128)S(1)} collective-permute-done((f32[128,128]{1,0:T(8,128)S(1)}, f32[128,128]{1,0:T(8,128)S(1)}, u32[]{:S(2)}, u32[]{:S(2)}) %collective-permute-start.1) | collective-permute-done | bytes 65568 | tf_op jit(solution)/shard_map/ppermute | solution.py:313
  30.0 3.2 %collective-permute-start.4 = (f32[128,128]{1,0:T(8,128)S(1)}, f32[128,128]{1,0:T(8,128)S(1)}, u32[]{:S(2)}, u32[]{:S(2)}) collective-permute-start(f32[128,128]{1,0:T(8,128)S(1)} %multiply_add_fusion.2), channel_id=1, source_target_pairs={{0,24},{4,28},{8,0},{12,4},{16,8},{20,12},{24,16},{28,20},{32,56},... | collective-permute-start | bytes 196616 | tf_op jit(solution)/shard_map/ppermute | solution.py:313
  33.2 0.8 %collective-permute-start.3 = (f32[128,128]{1,0:T(8,128)S(1)}, f32[128,128]{1,0:T(8,128)S(1)}, u32[]{:S(2)}, u32[]{:S(2)}) collective-permute-start(f32[128,128]{1,0:T(8,128)S(1)} %multiply_add_fusion.2), channel_id=1, source_target_pairs={{0,16},{4,20},{8,24},{12,28},{16,0},{20,4},{24,8},{28,12},{32,48},... | collective-permute-start | bytes 196616 | tf_op jit(solution)/shard_map/ppermute | solution.py:313
  34.0 0.9 %collective-permute-start.2 = (f32[128,128]{1,0:T(8,128)S(1)}, f32[128,128]{1,0:T(8,128)S(1)}, u32[]{:S(2)}, u32[]{:S(2)}) collective-permute-start(f32[128,128]{1,0:T(8,128)S(1)} %multiply_add_fusion.2), channel_id=1, source_target_pairs={{0,8},{4,12},{8,16},{12,20},{16,24},{20,28},{24,0},{28,4},{32,40},... | collective-permute-start | bytes 196616 | tf_op jit(solution)/shard_map/ppermute | solution.py:313
  34.9 2.7 %tables.1 = bf16[128,64,128]{2,1,0:T(8,128)(2,1)S(1)} custom-call(f32[16,1024]{1,0:T(8,128)S(1)} %copy-done.2, f32[16,1024]{1,0:T(8,128)S(1)} %copy-done.1, f32[1,1024]{1,0:T(1,128)S(1)} %bitcast.6), custom_call_target="tpu_custom_call" | custom-call | tf_op jit(solution)/shard_map/tables/pallas_call | solution.py:215
  37.6 1.4 %copy-done = bf16[128,64,128]{2,1,0:T(8,128)(2,1)} copy-done((bf16[128,64,128]{2,1,0:T(8,128)(2,1)}, bf16[128,64,128]{2,1,0:T(8,128)(2,1)S(1)}, u32[]{:S(2)}) %copy-start) | copy-done | bytes 2097176
  39.0 0.0 collective-permute-done.4
  39.0 0.0 collective-permute-done.3
  39.0 0.7 %collective-permute-done.2 = f32[128,128]{1,0:T(8,128)S(1)} collective-permute-done((f32[128,128]{1,0:T(8,128)S(1)}, f32[128,128]{1,0:T(8,128)S(1)}, u32[]{:S(2)}, u32[]{:S(2)}) %collective-permute-start.2) | collective-permute-done | bytes 65568 | tf_op jit(solution)/shard_map/ppermute | solution.py:313
  39.7 3.1 %collective-permute-start.7 = (f32[128,128]{1,0:T(8,128)S(1)}, f32[128,128]{1,0:T(8,128)S(1)}, u32[]{:S(2)}, u32[]{:S(2)}) collective-permute-start(f32[128,128]{1,0:T(8,128)S(1)} %multiply_add_fusion.1), channel_id=1, source_target_pairs={{0,96},{4,100},{8,104},{12,108},{16,112},{20,116},{24,120},{28,124... | collective-permute-start | bytes 196616 | tf_op jit(solution)/shard_map/ppermute | solution.py:313
  42.8 0.6 collective-permute-start.6
  43.4 1.0 %collective-permute-start.5 = (f32[128,128]{1,0:T(8,128)S(1)}, f32[128,128]{1,0:T(8,128)S(1)}, u32[]{:S(2)}, u32[]{:S(2)}) collective-permute-start(f32[128,128]{1,0:T(8,128)S(1)} %multiply_add_fusion.1), channel_id=1, source_target_pairs={{0,32},{4,36},{8,40},{12,44},{16,48},{20,52},{24,56},{28,60},{32,6... | collective-permute-start | bytes 196616 | tf_op jit(solution)/shard_map/ppermute | solution.py:313
  44.4 9.2 %query.1 = bf16[1024,2048]{1,0:T(8,128)(2,1)} custom-call(bf16[3,1024,2048]{2,1,0:T(8,128)(2,1)} %streams.3, bf16[3,1024,128]{2,1,0:T(8,128)(2,1)S(1)} %pad.4.rims, f32[1024,9]{1,0:T(8,128)S(1)} %bitcast.4), custom_call_target="tpu_custom_call" | custom-call | flops 2147483648 | bytes 8388608 | tf_op jit(solution)/shard_map/query/pallas_call | solution.py:225
  53.6 0.0 collective-permute-done.7
  53.6 0.0 collective-permute-done.6
  53.6 0.1 multiply_add_fusion.before
  53.7 14.4 %mix.1 = bf16[1024,2048]{1,0:T(8,128)(2,1)} custom-call(bf16[128,128,128]{2,1,0:T(8,128)(2,1)} %get-tuple-element.8.gated, f32[128,8,128]{2,1,0:T(8,128)S(1)} %get-tuple-element.9.sums, bf16[1024,2048]{1,0:T(8,128)(2,1)} %query.1, f32[128,128]{1,0:T(8,128)S(1)} %reshape.7.rates, bf16[128,64,128]{2,1,0:T(8,128)(2,1)} %copy-done, ...), custom_call_target="tpu_custom_call" | custom-call | tf_op jit(solution)/shard_map/mix/pallas_call | solution.py:275
  (7 shorter events, 0.1 us)
Async XLA Ops:
  1.7 6.2 %collective-permute-start = (bf16[3,1024,2]{1,2,0:T(2,128)(2,1)S(1)}, bf16[3,1024,2]{1,2,0:T(2,128)(2,1)S(1)}, u32[]{:S(2)}, u32[]{:S(2)}) collective-permute-start(bf16[3,1024,2]{1,2,0:T(2,128)(2,1)S(1)} %copy.14), channel_id=1, source_target_pairs={{0,4},{4,8},{8,12},{12,16},{16,20},{20,24},{24,28},{28,32},{32,36}... | collective-permute-start | bytes 36872 | tf_op jit(solution)/shard_map/ppermute | solution.py:338
  8.7 26.2 %copy-start.1 = (f32[16,1024]{1,0:T(8,128)S(1)}, f32[16,1024]{1,0:T(8,128)}, u32[]{:S(2)}) copy-start(f32[16,1024]{1,0:T(8,128)} %rates.1) | copy-start | bytes 196612
  8.7 26.2 %copy-start.2 = (f32[16,1024]{1,0:T(8,128)S(1)}, f32[16,1024]{1,0:T(8,128)}, u32[]{:S(2)}) copy-start(f32[16,1024]{1,0:T(8,128)} %residues.1) | copy-start | bytes 196612
  8.7 26.2 %copy-start.3 = (f32[1024]{0:T(1024)S(1)}, f32[1024]{0:T(1024)}, u32[]{:S(2)}) copy-start(f32[1024]{0:T(1024)} %param.9) | copy-start | bytes 12292
  25.7 4.3 %collective-permute-start.1 = (f32[128,128]{1,0:T(8,128)S(1)}, f32[128,128]{1,0:T(8,128)S(1)}, u32[]{:S(2)}, u32[]{:S(2)}) collective-permute-start(f32[128,128]{1,0:T(8,128)S(1)} %get-tuple-element.10), channel_id=1, source_target_pairs={{0,4},{4,0},{8,12},{12,8},{16,20},{20,16},{24,28},{28,24},{32,36},... | collective-permute-start | bytes 196616 | tf_op jit(solution)/shard_map/ppermute | solution.py:313
  30.0 9.0 %collective-permute-start.4 = (f32[128,128]{1,0:T(8,128)S(1)}, f32[128,128]{1,0:T(8,128)S(1)}, u32[]{:S(2)}, u32[]{:S(2)}) collective-permute-start(f32[128,128]{1,0:T(8,128)S(1)} %multiply_add_fusion.2), channel_id=1, source_target_pairs={{0,24},{4,28},{8,0},{12,4},{16,8},{20,12},{24,16},{28,20},{32,56},... | collective-permute-start | bytes 196616 | tf_op jit(solution)/shard_map/ppermute | solution.py:313
  33.2 5.8 %collective-permute-start.3 = (f32[128,128]{1,0:T(8,128)S(1)}, f32[128,128]{1,0:T(8,128)S(1)}, u32[]{:S(2)}, u32[]{:S(2)}) collective-permute-start(f32[128,128]{1,0:T(8,128)S(1)} %multiply_add_fusion.2), channel_id=1, source_target_pairs={{0,16},{4,20},{8,24},{12,28},{16,0},{20,4},{24,8},{28,12},{32,48},... | collective-permute-start | bytes 196616 | tf_op jit(solution)/shard_map/ppermute | solution.py:313
  34.0 5.7 %collective-permute-start.2 = (f32[128,128]{1,0:T(8,128)S(1)}, f32[128,128]{1,0:T(8,128)S(1)}, u32[]{:S(2)}, u32[]{:S(2)}) collective-permute-start(f32[128,128]{1,0:T(8,128)S(1)} %multiply_add_fusion.2), channel_id=1, source_target_pairs={{0,8},{4,12},{8,16},{12,20},{16,24},{20,28},{24,0},{28,4},{32,40},... | collective-permute-start | bytes 196616 | tf_op jit(solution)/shard_map/ppermute | solution.py:313
  37.6 1.4 %copy-start = (bf16[128,64,128]{2,1,0:T(8,128)(2,1)}, bf16[128,64,128]{2,1,0:T(8,128)(2,1)S(1)}, u32[]{:S(2)}) copy-start(bf16[128,64,128]{2,1,0:T(8,128)(2,1)S(1)} %tables.1) | copy-start | bytes 6291460
  39.7 13.9 %collective-permute-start.7 = (f32[128,128]{1,0:T(8,128)S(1)}, f32[128,128]{1,0:T(8,128)S(1)}, u32[]{:S(2)}, u32[]{:S(2)}) collective-permute-start(f32[128,128]{1,0:T(8,128)S(1)} %multiply_add_fusion.1), channel_id=1, source_target_pairs={{0,96},{4,100},{8,104},{12,108},{16,112},{20,116},{24,120},{28,124... | collective-permute-start | bytes 196616 | tf_op jit(solution)/shard_map/ppermute | solution.py:313
  42.8 10.8 %collective-permute-start.6 = (f32[128,128]{1,0:T(8,128)S(1)}, f32[128,128]{1,0:T(8,128)S(1)}, u32[]{:S(2)}, u32[]{:S(2)}) collective-permute-start(f32[128,128]{1,0:T(8,128)S(1)} %multiply_add_fusion.1), channel_id=1, source_target_pairs={{0,64},{4,68},{8,72},{12,76},{16,80},{20,84},{24,88},{28,92},{32,9... | collective-permute-start | bytes 196616 | tf_op jit(solution)/shard_map/ppermute | solution.py:313
  43.4 10.2 %collective-permute-start.5 = (f32[128,128]{1,0:T(8,128)S(1)}, f32[128,128]{1,0:T(8,128)S(1)}, u32[]{:S(2)}, u32[]{:S(2)}) collective-permute-start(f32[128,128]{1,0:T(8,128)S(1)} %multiply_add_fusion.1), channel_id=1, source_target_pairs={{0,32},{4,36},{8,40},{12,44},{16,48},{20,52},{24,56},{28,60},{32,6... | collective-permute-start | bytes 196616 | tf_op jit(solution)/shard_map/ppermute | solution.py:313

commit v2 on v1

v2 whole, which is shorter than its diff:
```python
import jax
import jax.numpy as jnp
from jax import lax
from jax.experimental import pallas as pl
from jax.experimental.pallas import tpu as pltpu
from jax.sharding import PartitionSpec as P

F32 = jnp.float32
BF16 = jnp.bfloat16
BATCH = 2
WIDE = 8
SHORT = 3
MODES = 16
GROUP = 8
STEP = 16
LANES = 128
MIB = 1024 * 1024


def cat(parts, axis=0):
    return jnp.concatenate(parts, axis=axis)


def iota(shape, dim):
    return lax.broadcasted_iota(jnp.int32, shape, dim)


def split(x):
    high = x.astype(BF16)
    return high, (x - high.astype(F32)).astype(BF16)


def filtered(load, rim, taps, count):
    lane = iota((16, LANES), 1)
    first, second = lane < 1, lane < 2
    before1, before2 = pltpu.roll(rim, 1, 1), pltpu.roll(rim, 2, 1)
    for k in range(count):
        here = load(k)
        turned1, turned2 = pltpu.roll(here, 1, 1), pltpu.roll(here, 2, 1)
        back1 = jnp.where(first, before1, turned1)
        back2 = jnp.where(second, before2, turned2)
        yield taps[0] * here.astype(F32) + taps[1] * back1.astype(F32) + taps[2] * back2.astype(F32)
        before1, before2 = turned1, turned2


def swap_blocks(tiles):
    lane = iota(tiles[0].shape, 1) // STEP
    tiles = [pltpu.roll(x, STEP * c, 1) if c else x for c, x in enumerate(tiles)]
    for d in (4, 2, 1):
        keep = (lane & d) == 0
        tiles = [jnp.where(keep, tiles[j], tiles[(j + d) % 8]) for j in range(8)]
    tiles = [tiles[-j % 8] for j in range(8)]
    return [pltpu.roll(x, LANES - STEP * j, 1) if j else x for j, x in enumerate(tiles)]


def spread(base):
    lane = iota(base.shape, 1) // STEP
    return cat([jnp.where(lane == c, base, jnp.zeros_like(base)) for c in range(GROUP)], 0)


def decay_in(rate):
    row = iota((STEP, LANES), 0).astype(F32)
    high, low = split(jnp.exp(rate * (row - float(STEP))))
    return cat([spread(high), spread(low)], 0)


def table_kernel(residues, rates, skips, tables):
    lane = iota((STEP, LANES), 1)
    place = (lane % STEP).astype(F32)
    row = iota((STEP, LANES), 0)
    after = (lane % STEP) >= row
    same = (lane % STEP) == row

    def tile(i, _):
        cols = pl.ds(pl.multiple_of(i * LANES, LANES), LANES)
        rate16, residue16 = rates[:, cols], residues[:, cols]
        weight16 = residue16 * jnp.sqrt(2.0 * rate16)
        skip16 = jnp.broadcast_to(skips[:, cols], (STEP, LANES))
        for j in range(LANES // GROUP):
            at = lane // STEP + GROUP * j
            rate = jnp.take_along_axis(rate16, at, axis=1)
            weight = jnp.take_along_axis(weight16, at, axis=1)
            skip = jnp.take_along_axis(skip16, at, axis=1)
            out = weight * jnp.exp(-rate * place)
            taps = jnp.broadcast_to(jnp.sum(out, axis=0, keepdims=True), (STEP, LANES))
            near = pltpu.roll(taps, 0, 1, stride=1, stride_axis=0)
            near = jnp.where(after, near, 0.0) + jnp.where(same, skip, 0.0)
            g = i * (LANES // GROUP) + j
            tables[g] = cat([*split(out), *split(near)], 0)
        return 0

    lax.fori_loop(0, rates.shape[1] // LANES, tile, 0)


def moves(source, target, semaphores, rows, dim=0):
    def copy(i):
        block = (slice(None),) * dim + (pl.ds(pl.multiple_of(i * rows, rows), rows),)
        return pltpu.make_async_copy(source.at[block], target.at[block], semaphores.at[i])

    return copy


def step_decay(rates, at, count, times):
    return jnp.exp(-float(times) * rates[pl.ds(at, count), :])[:, None, :]


def gate_kernel(source, rims, taps, rates, gated_out, sums_out, state, streams, gated, sums, xs, zs, arrived, sent, sent_sums):
    tiles = streams.shape[2] // LANES
    pairs = streams.shape[1] // 16
    segment = streams.shape[2] // 8
    unroll = zs.shape[0] // 2
    steps = pairs // unroll
    fetch = moves(source.at[pl.ds(1, 2)], streams, arrived, 16 * unroll, 1)
    send = moves(gated, gated_out, sent, 2 * unroll)
    send_sums = moves(sums, sums_out, sent_sums, 2 * unroll)
    for i in range(steps):
        fetch(i).start()
    left = 7.0 - iota((1, 8, LANES), 1).astype(F32)

    def step(i, _):
        fetch(i).wait()
        first = pl.multiple_of(i * 2 * unroll, 2 * unroll)
        for u in range(unroll):
            rows = pl.ds(pl.multiple_of((i * unroll + u) * 16, 16), 16)
            sides = []
            for s in (0, 1):
                tap = [
                    jnp.broadcast_to(taps[rows, pl.ds(3 * (s + 1) + j, 1)], (16, LANES)) for j in range(SHORT)
                ]
                load = lambda k, s=s, rows=rows: streams[s, rows, pl.ds(k * LANES, LANES)].astype(F32)
                sides.append(filtered(load, rims[s + 1, rows, :].astype(F32), tap, tiles))
            for k, (a, b) in enumerate(zip(*sides)):
                xs[pl.ds((u * 2 + k % 2) * LANES + k // 2 * 16, 16), :] = a * b
        for u in range(0, unroll, BATCH):
            for half in (0, 1):
                lined = swap_blocks(
                    [xs[pl.ds(u * 256 + 8 * half + c, 16 * BATCH, stride=16), :] for c in range(GROUP)]
                )
                for w in range(BATCH):
                    gated[first + 2 * (u + w) + half] = cat(
                        [tile[16 * w : 16 * w + 16] for tile in lined], 0
                    ).astype(BF16)
        for v in range(2 * unroll):
            x = gated[first + v]
            zs[v] = jnp.dot(
                cat([x, x], 1), decay_in(rates[pl.ds(first + v, 1), :]), preferred_element_type=F32
            )
        for v in range(0, 2 * unroll, WIDE):
            some = pl.ds(first + v, WIDE)
            over = jnp.broadcast_to(step_decay(rates, first + v, WIDE, STEP), (WIDE, 8, LANES))
            held = zs[v : v + WIDE, 0:8, :]
            for k in range(1, 16):
                at = 16 * (k % 8) + 8 * (k // 8)
                held = held * over + zs[v : v + WIDE, at : at + 8, :]
            sums[some] = held
            rate = rates[some, :][:, None, :]
            state[some, :] = jnp.sum(held * jnp.exp(-float(segment) * rate * left), axis=1)
        send(i).start()
        send_sums(i).start()
        return 0

    lax.fori_loop(0, steps, step, 0)
    for i in range(steps):
        send(i).wait()
        send_sums(i).wait()


def query_kernel(source, rims, taps, query_out, streams, query, arrived, sent):
    tiles = streams.shape[2] // LANES
    unroll = 4
    steps = streams.shape[1] // 16 // unroll
    fetch = moves(source.at[pl.ds(0, 1)], streams, arrived, 16 * unroll, 1)
    send = moves(query, query_out, sent, 16 * unroll)
    for i in range(steps):
        fetch(i).start()

    def step(i, _):
        fetch(i).wait()
        for u in range(unroll):
            rows = pl.ds(pl.multiple_of((i * unroll + u) * 16, 16), 16)
            tap = [jnp.broadcast_to(taps[rows, pl.ds(j, 1)], (16, LANES)) for j in range(SHORT)]
            load = lambda k, rows=rows: streams[0, rows, pl.ds(k * LANES, LANES)].astype(F32)
            for k, tile in enumerate(filtered(load, rims[0, rows, :].astype(F32), tap, tiles)):
                query[rows, pl.ds(k * LANES, LANES)] = tile.astype(BF16)
        send(i).start()
        return 0

    lax.fori_loop(0, steps, step, 0)
    for i in range(steps):
        send(i).wait()


def mix_kernel(gated_in, sums_in, query_in, rates, tables_in, before, target, gated, sums, query, tables, out, ys, zs, arrived, sent):
    tiles = query.shape[1] // LANES
    pairs = query.shape[0] // 16
    segment = query.shape[1] // 8
    unroll = zs.shape[1]
    row = iota((WIDE, 8, LANES), 1)

    steps = pairs // unroll
    inputs = (
        moves(gated_in, gated, arrived.at[0], 2 * unroll),
        moves(sums_in, sums, arrived.at[1], 2 * unroll),
        moves(tables_in, tables, arrived.at[2], 2 * unroll),
        moves(query_in, query, arrived.at[3], 16 * unroll),
    )
    send = moves(out, target, sent, 16 * unroll)
    for i in range(steps):
        for copy in inputs:
            copy(i).start()

    def step(i, _):
        for copy in inputs:
            copy(i).wait()
        base_group = pl.multiple_of(i * 2 * unroll, 2 * unroll)
        for v in range(2 * unroll):
            x = gated[base_group + v]
            zs[v % 2, v // 2] = jnp.dot(
                cat([x, x], 1), decay_in(rates[pl.ds(base_group + v, 1), :]), preferred_element_type=F32
            )
        for v in range(0, 2 * unroll, WIDE):
            some = pl.ds(base_group + v, WIDE)
            over = jnp.broadcast_to(step_decay(rates, base_group + v, WIDE, STEP), (WIDE, 8, LANES))
            entry = jnp.broadcast_to(before[some, :][:, None, :], (WIDE, 8, LANES))
            held = jnp.where(row == 0, entry, pltpu.roll(sums[some], 1, 1))
            for d in (1, 2, 4):
                earlier = jnp.where(row < d, 0.0, pltpu.roll(held, d, 1))
                held = held + step_decay(rates, base_group + v, WIDE, segment * d) * earlier
            held = [held[w] for w in range(WIDE)]
            for k in range(16):
                at = 16 * (k % 8) + 8 * (k // 8)
                for w in range(WIDE):
                    z = zs.at[(v + w) % 2, (v + w) // 2, pl.ds(at, 8)]
                    entering = z[...]
                    z[...] = held[w]
                    held[w] = held[w] * over[w] + entering
        for v in range(2 * unroll):
            x = gated[base_group + v]
            high, low = split(zs[v % 2, v // 2])
            base = tables[base_group + v]
            far_high, far_low, near_high, near_low = [spread(base[16 * n : 16 * n + 16]) for n in range(4)]
            zs[v % 2, v // 2] = jnp.dot(
                cat([high, high, low, x, x], 1),
                cat([far_high, far_low, far_high, near_high, near_low], 0),
                preferred_element_type=F32,
            )
        for u in range(0, unroll, 2 * BATCH):
            for half in (0, 1):
                for odd in (0, 1):
                    lined = swap_blocks(
                        [
                            zs[half, u : u + 2 * BATCH, 16 * b + 8 * odd : 16 * b + 8 * odd + 8, :].reshape(16 * BATCH, LANES)
                            for b in range(8)
                        ]
                    )
                    for c in range(GROUP):
                        ys[pl.ds((odd * unroll + u) * LANES + 8 * half + c, 16 * BATCH, stride=16), :] = lined[c]
        for u in range(unroll):
            rows = pl.ds(pl.multiple_of((i * unroll + u) * 16, 16), 16)
            for k in range(tiles):
                mixed = ys[pl.ds((k % 2 * unroll + u) * LANES + k // 2 * 16, 16), :].astype(BF16)
                cols = pl.ds(k * LANES, LANES)
                out[rows, cols] = query[rows, cols] * mixed
        send(i).start()
        return 0

    lax.fori_loop(0, steps, step, 0)
    for i in range(steps):
        send(i).wait()


def make_tables(residues, rates, skip):
    channels = rates.shape[1]
    groups = channels // GROUP
    return pl.pallas_call(
        table_kernel,
        out_shape=jax.ShapeDtypeStruct((groups, 4 * STEP, LANES), BF16),
        compiler_params=pltpu.CompilerParams(vmem_limit_bytes=8 * MIB),
        name="tables",
    )(residues, rates, skip[None, :])


WHOLE = pl.BlockSpec(memory_space=pltpu.VMEM)
APART = pl.BlockSpec(memory_space=pltpu.HBM)


def make_query(streams, rims, taps):
    channels, length = streams.shape[1:]
    return pl.pallas_call(
        query_kernel,
        in_specs=[APART, WHOLE, WHOLE],
        out_specs=APART,
        out_shape=jax.ShapeDtypeStruct((channels, length), BF16),
        scratch_shapes=[
            pltpu.VMEM((1, channels, length), BF16),
            pltpu.VMEM((channels, length), BF16),
            pltpu.SemaphoreType.DMA((channels // 64,)),
            pltpu.SemaphoreType.DMA((channels // 64,)),
        ],
        compiler_params=pltpu.CompilerParams(vmem_limit_bytes=50 * MIB),
        name="query",
    )(streams, rims, taps)


def gate(streams, rims, taps, rates, unroll=8):
    channels, length = streams.shape[1:]
    groups = channels // GROUP
    rows = length // STEP
    return pl.pallas_call(
        gate_kernel,
        in_specs=[APART, WHOLE, WHOLE, WHOLE],
        out_specs=[APART, APART, WHOLE],
        out_shape=[
            jax.ShapeDtypeStruct((groups, rows, LANES), BF16),
            jax.ShapeDtypeStruct((groups, 8, LANES), F32),
            jax.ShapeDtypeStruct((groups, LANES), F32),
        ],
        scratch_shapes=[
            pltpu.VMEM((2, channels, length), BF16),
            pltpu.VMEM((groups, rows, LANES), BF16),
            pltpu.VMEM((groups, 8, LANES), F32),
            pltpu.VMEM((unroll * 2 * rows, LANES), F32),
            pltpu.VMEM((2 * unroll, rows, LANES), F32),
            pltpu.SemaphoreType.DMA((channels // (16 * unroll),)),
            pltpu.SemaphoreType.DMA((channels // (16 * unroll),)),
            pltpu.SemaphoreType.DMA((channels // (16 * unroll),)),
        ],
        compiler_params=pltpu.CompilerParams(vmem_limit_bytes=50 * MIB),
        name="gate",
    )(streams, rims, taps, rates)


def mix(gated, sums, query, rates, tables, before, unroll=16):
    channels, length = query.shape
    rows = length // STEP
    return pl.pallas_call(
        mix_kernel,
        in_specs=[APART, APART, APART, WHOLE, APART, WHOLE],
        out_specs=APART,
        out_shape=jax.ShapeDtypeStruct((channels, length), BF16),
        scratch_shapes=[
            pltpu.VMEM(gated.shape, BF16),
            pltpu.VMEM(sums.shape, F32),
            pltpu.VMEM((channels, length), BF16),
            pltpu.VMEM(tables.shape, BF16),
            pltpu.VMEM((channels, length), BF16),
            pltpu.VMEM((unroll * 2 * rows, LANES), F32),
            pltpu.VMEM((2, unroll, rows, LANES), F32),
            pltpu.SemaphoreType.DMA((4, channels // (16 * unroll))),
            pltpu.SemaphoreType.DMA((channels // (16 * unroll),)),
        ],
        compiler_params=pltpu.CompilerParams(vmem_limit_bytes=50 * MIB),
        name="mix",
    )(gated, sums, query, rates, tables, before)


def states_before(state, rates, length, beside):
    axis = "ctx"
    index = lax.axis_index(axis)
    devices = lax.axis_size(axis)

    def decay(times):
        return jnp.exp(-float(length) * rates * jnp.asarray(times, F32))

    before = jnp.zeros_like(state)
    total = state
    span = 1
    made = []
    for size, work in zip((2, 4, 4), beside):
        place = (index // span) % size

        def moved(by):
            pairs = []
            for i in range(devices):
                at = (i // span) % size
                pairs.append((i, i + ((at + by) % size - at) * span))
            return lax.ppermute(total, axis, pairs)

        others = [moved(by) for by in range(1, size)]
        prefix = jnp.zeros_like(state)
        whole = decay(span * (size - 1 - place)) * total
        for by, other in enumerate(others, 1):
            at = (place - by) % size
            valid = by <= place
            prefix = prefix + jnp.where(valid, decay(span * jnp.where(valid, by - 1, 0)) * other, 0.0)
            whole = whole + decay(span * (size - 1 - at)) * other
        before = before + decay(index % span) * prefix
        total = whole
        if work is not None:
            total, work = lax.optimization_barrier((total, work))
            made.append(work)
        span *= size
    return before, made


def on_device(streams, short_filters, residues, rates, skip):
    channels, length = streams.shape[1:]
    groups = channels // GROUP

    def by_group(x):
        return x.T.reshape(groups, GROUP * MODES)

    devices = lax.axis_size("ctx")
    edge = streams[:, :, length - (SHORT - 1) :]
    rims = lax.ppermute(edge, "ctx", [(i, i + 1) for i in range(devices - 1)])
    rims = jnp.pad(rims, ((0, 0), (0, 0), (LANES - (SHORT - 1), 0)))
    taps = short_filters.reshape(9, channels).T
    rate = by_group(rates)
    gated, sums, state = gate(streams, rims, taps, rate)
    tables = make_tables(residues, rates, skip)
    query = make_query(streams, rims, taps)
    before, (query,) = states_before(state, rate, length, (None, query, None))
    return mix(gated, sums, query, rate, tables, before)


def solution(mesh):
    in_specs = (P(None, "tp", "ctx"), P(None, None, "tp"), P(None, "tp"), P(None, "tp"), P("tp"))
    out_specs = P("tp", "ctx")
    return jax.shard_map(
        on_device, mesh=mesh, in_specs=in_specs, out_specs=out_specs, check_vma=False
    )
```

time: 69 us -> 65.2 us (0.945)
  Pallas kernels: 43.4 us -> 39.2 us
  waiting for transfers between devices: 3.6 us -> 5.05 us
  local copies, waits for them, and re-layouts: 6.08 us -> 4.71 us
    pallas_call x3, Pallas kernels: 40.7 us -> 36.5 us  [the longest x1 17.2 us: gate(): pl.pallas_call(gate_kernel, in_specs=[APART, WHOLE, WHOLE, WHOLE], out_sp...]
    ppermute x7, waiting for transfers between devices: 3.59 us -> 5.04 us  [moved(): return lax.ppermute(total, axis, pairs)]
    unnamed x9 -> x7, local copies, waits for them, and re-layouts: 1.68 us -> 0.31 us
  transfers between devices with their start and end apart: 8 -> 8, of which waited for: 2 -> 3; matrix products, arithmetic and copies ran while one was open for 3% -> 4% of each run, Pallas kernels for 17% -> 14%
where the time goes in v2:
time: 65.2 us; the launch traced here: 64.2 us
  Pallas kernels  39.2 us (60%)
  starting transfers between devices  14.9 us (23%)
  waiting for transfers between devices  5.05 us (8%)
  local copies, waits for them, and re-layouts  4.71 us (7%)
    pallas_call x1, Pallas kernels, gate(): pl.pallas_call(gate_kernel, in_specs=[APART, WHOLE, WHOLE, WHOLE], out_sp...  17.2 us
    pallas_call x1, Pallas kernels, mix(): pl.pallas_call(mix_kernel, in_specs=[APART, APART, APART, WHOLE, APART, W...  12.9 us
    ppermute x7, starting transfers between devices, moved(): return lax.ppermute(total, axis, pairs)  11 us
    pallas_call x1, Pallas kernels, make_query(): pl.pallas_call(query_kernel, in_specs=[APART, WHOLE, WHOLE], out_specs=AP...  6.41 us
    ppermute x7, waiting for transfers between devices, moved(): return lax.ppermute(total, axis, pairs)  5.04 us
    ppermute x1, starting transfers between devices, on_device(): rims = lax.ppermute(edge, 'ctx', [(i, i + 1) for i in range(devices - 1)])  3.9 us
    pallas_call x1, Pallas kernels, make_tables(): pl.pallas_call(table_kernel, out_shape=jax.ShapeDtypeStruct((groups, 4 *...  2.69 us
    slice x1, local copies, waits for them, and re-layouts, on_device(): edge = streams[:, :, length - (SHORT - 1):]  1.41 us
  transfers between devices with their start and end apart: 8, of which 3 were waited for; matrix products, arithmetic and copies ran while one was open for 4% of the time, Pallas kernels for 14%

profile of v2, /device:TPU:0, one launch (start us, length us, event | category | flops | bytes accessed | tf_op | source)
XLA Modules:
  0.0 64.2 jit_solution(12247349028036868080)
XLA Ops:
  0.0 1.4 %slice.3 = bf16[3,1024,2]{2,1,0:T(8,128)(2,1)S(1)} slice(bf16[3,1024,2048]{2,1,0:T(8,128)(2,1)} %source.3), slice={[0:3], [0:1024], [2046:2048]} | slice | bytes 24576 | tf_op jit(solution)/shard_map/slice | solution.py:404
  1.4 0.3 copy.14
  1.7 3.9 %collective-permute-start = (bf16[3,1024,2]{1,2,0:T(2,128)(2,1)S(1)}, bf16[3,1024,2]{1,2,0:T(2,128)(2,1)S(1)}, u32[]{:S(2)}, u32[]{:S(2)}) collective-permute-start(bf16[3,1024,2]{1,2,0:T(2,128)(2,1)S(1)} %copy.14), channel_id=1, source_target_pairs={{0,4},{4,8},{8,12},{12,16},{16,20},{20,24},{24,28},{28,32},{32,36}... | collective-permute-start | bytes 36872 | tf_op jit(solution)/shard_map/ppermute | solution.py:405
  5.6 0.8 %reshape.6 = f32[9,1024]{1,0:T(8,128)S(1)} reshape(f32[3,3,1024]{2,1,0:T(4,128)} %param.6) | data formatting | bytes 73728 | tf_op jit(solution)/shard_map/reshape | solution.py:407
  6.4 0.2 copy.12
  6.7 1.0 %copy.13 = f32[1024,16]{1,0:T(8,128)S(1)} copy(f32[1024,16]{0,1:T(8,128)} %bitcast.5) | data formatting | bytes 131072 | tf_op jit(solution)/shard_map/transpose | solution.py:401
  7.7 0.2 reshape.7.rates
  7.9 0.0 collective-permute-done
  7.9 0.4 copy.11
  8.3 0.3 pad.4.rims
  8.7 17.2 %gate.1 = (bf16[128,128,128]{2,1,0:T(8,128)(2,1)}, f32[128,8,128]{2,1,0:T(8,128)S(1)}, f32[128,128]{1,0:T(8,128)S(1)}) custom-call(bf16[3,1024,2048]{2,1,0:T(8,128)(2,1)} %source.3, bf16[3,1024,128]{2,1,0:T(8,128)(2,1)S(1)} %pad.4.rims, f32[1024,9]{1,0:T(8,128)S(1)} %bitcast.3, f32[128,128]{1,0:T(8,128)S(1)} %reshape.7.rates), custom_call_target="tpu_custom_call" | custom-call | tf_op jit(solution)/shard_map/gate/pallas_call | solution.py:309
  25.9 1.5 %collective-permute-start.1 = (f32[128,128]{1,0:T(8,128)S(1)}, f32[128,128]{1,0:T(8,128)S(1)}, u32[]{:S(2)}, u32[]{:S(2)}) collective-permute-start(f32[128,128]{1,0:T(8,128)S(1)} %get-tuple-element.12), channel_id=1, source_target_pairs={{0,4},{4,0},{8,12},{12,8},{16,20},{20,16},{24,28},{28,24},{32,36},... | collective-permute-start | bytes 196616 | tf_op jit(solution)/shard_map/ppermute | solution.py:377
  27.4 2.9 %collective-permute-done.1 = f32[128,128]{1,0:T(8,128)S(1)} collective-permute-done((f32[128,128]{1,0:T(8,128)S(1)}, f32[128,128]{1,0:T(8,128)S(1)}, u32[]{:S(2)}, u32[]{:S(2)}) %collective-permute-start.1) | collective-permute-done | bytes 65568 | tf_op jit(solution)/shard_map/ppermute | solution.py:377
  30.3 3.2 %collective-permute-start.4 = (f32[128,128]{1,0:T(8,128)S(1)}, f32[128,128]{1,0:T(8,128)S(1)}, u32[]{:S(2)}, u32[]{:S(2)}) collective-permute-start(f32[128,128]{1,0:T(8,128)S(1)} %multiply_add_fusion.2), channel_id=1, source_target_pairs={{0,24},{4,28},{8,0},{12,4},{16,8},{20,12},{24,16},{28,20},{32,56},... | collective-permute-start | bytes 196616 | tf_op jit(solution)/shard_map/ppermute | solution.py:377
  33.5 0.8 %collective-permute-start.3 = (f32[128,128]{1,0:T(8,128)S(1)}, f32[128,128]{1,0:T(8,128)S(1)}, u32[]{:S(2)}, u32[]{:S(2)}) collective-permute-start(f32[128,128]{1,0:T(8,128)S(1)} %multiply_add_fusion.2), channel_id=1, source_target_pairs={{0,16},{4,20},{8,24},{12,28},{16,0},{20,4},{24,8},{28,12},{32,48},... | collective-permute-start | bytes 196616 | tf_op jit(solution)/shard_map/ppermute | solution.py:377
  34.3 0.9 %collective-permute-start.2 = (f32[128,128]{1,0:T(8,128)S(1)}, f32[128,128]{1,0:T(8,128)S(1)}, u32[]{:S(2)}, u32[]{:S(2)}) collective-permute-start(f32[128,128]{1,0:T(8,128)S(1)} %multiply_add_fusion.2), channel_id=1, source_target_pairs={{0,8},{4,12},{8,16},{12,20},{16,24},{20,28},{24,0},{28,4},{32,40},... | collective-permute-start | bytes 196616 | tf_op jit(solution)/shard_map/ppermute | solution.py:377
  35.1 6.4 %query.1.query_in = bf16[1024,2048]{1,0:T(8,128)(2,1)} custom-call(bf16[3,1024,2048]{2,1,0:T(8,128)(2,1)} %source.3, bf16[3,1024,128]{2,1,0:T(8,128)(2,1)S(1)} %pad.4.rims, f32[1024,9]{1,0:T(8,128)S(1)} %bitcast.4), custom_call_target="tpu_custom_call" | custom-call | tf_op jit(solution)/shard_map/query/pallas_call | solution.py:289
  41.6 0.0 collective-permute-done.4
  41.6 0.0 collective-permute-done.3
  41.6 0.0 collective-permute-done.2
  41.6 0.1 multiply_add_fusion.1
  41.7 3.1 %collective-permute-start.7 = (f32[128,128]{1,0:T(8,128)S(1)}, f32[128,128]{1,0:T(8,128)S(1)}, u32[]{:S(2)}, u32[]{:S(2)}) collective-permute-start(f32[128,128]{1,0:T(8,128)S(1)} %multiply_add_fusion.1), channel_id=1, source_target_pairs={{0,96},{4,100},{8,104},{12,108},{16,112},{20,116},{24,120},{28,124... | collective-permute-start | bytes 196616 | tf_op jit(solution)/shard_map/ppermute | solution.py:377
  44.7 0.6 collective-permute-start.6
  45.4 1.0 %collective-permute-start.5 = (f32[128,128]{1,0:T(8,128)S(1)}, f32[128,128]{1,0:T(8,128)S(1)}, u32[]{:S(2)}, u32[]{:S(2)}) collective-permute-start(f32[128,128]{1,0:T(8,128)S(1)} %multiply_add_fusion.1), channel_id=1, source_target_pairs={{0,32},{4,36},{8,40},{12,44},{16,48},{20,52},{24,56},{28,60},{32,6... | collective-permute-start | bytes 196616 | tf_op jit(solution)/shard_map/ppermute | solution.py:377
  46.3 0.0 copy-done
  46.3 0.0 copy-done.1
  46.4 2.7 %tables.1.tables_in = bf16[128,64,128]{2,1,0:T(8,128)(2,1)S(1)} custom-call(f32[16,1024]{1,0:T(8,128)S(1)} %copy-done.1, f32[16,1024]{1,0:T(8,128)S(1)} %copy-done, f32[1,1024]{1,0:T(1,128)S(1)} %bitcast.6), custom_call_target="tpu_custom_call" | custom-call | tf_op jit(solution)/shard_map/tables/pallas_call | solution.py:275
  49.1 0.0 collective-permute-done.7
  49.1 1.5 %collective-permute-done.6 = f32[128,128]{1,0:T(8,128)S(1)} collective-permute-done((f32[128,128]{1,0:T(8,128)S(1)}, f32[128,128]{1,0:T(8,128)S(1)}, u32[]{:S(2)}, u32[]{:S(2)}) %collective-permute-start.6) | collective-permute-done | bytes 65568 | tf_op jit(solution)/shard_map/ppermute | solution.py:377
  50.6 0.7 %collective-permute-done.5 = f32[128,128]{1,0:T(8,128)S(1)} collective-permute-done((f32[128,128]{1,0:T(8,128)S(1)}, f32[128,128]{1,0:T(8,128)S(1)}, u32[]{:S(2)}, u32[]{:S(2)}) %collective-permute-start.5) | collective-permute-done | bytes 65568 | tf_op jit(solution)/shard_map/ppermute | solution.py:377
  51.2 0.1 multiply_add_fusion.before
  51.3 12.9 %mix.1 = bf16[1024,2048]{1,0:T(8,128)(2,1)} custom-call(bf16[128,128,128]{2,1,0:T(8,128)(2,1)} %get-tuple-element.10.gated_in, f32[128,8,128]{2,1,0:T(8,128)S(1)} %get-tuple-element.11.sums_in, bf16[1024,2048]{1,0:T(8,128)(2,1)} %query.1.query_in, f32[128,128]{1,0:T(8,128)S(1)} %reshape.7.rates, bf16[128,64,128]{2,1,0:T(8,128)(2,1)S(1)} %tables.1.tables_in, ...), custom_call_target="tpu_custom_call" | custom-call | tf_op jit(solution)/shard_map/mix/pallas_call | solution.py:336
  (5 shorter events, 0.0 us)
Async XLA Ops:
  1.7 6.2 %collective-permute-start = (bf16[3,1024,2]{1,2,0:T(2,128)(2,1)S(1)}, bf16[3,1024,2]{1,2,0:T(2,128)(2,1)S(1)}, u32[]{:S(2)}, u32[]{:S(2)}) collective-permute-start(bf16[3,1024,2]{1,2,0:T(2,128)(2,1)S(1)} %copy.14), channel_id=1, source_target_pairs={{0,4},{4,8},{8,12},{12,16},{16,20},{20,24},{24,28},{28,32},{32,36}... | collective-permute-start | bytes 36872 | tf_op jit(solution)/shard_map/ppermute | solution.py:405
  25.9 4.3 %collective-permute-start.1 = (f32[128,128]{1,0:T(8,128)S(1)}, f32[128,128]{1,0:T(8,128)S(1)}, u32[]{:S(2)}, u32[]{:S(2)}) collective-permute-start(f32[128,128]{1,0:T(8,128)S(1)} %get-tuple-element.12), channel_id=1, source_target_pairs={{0,4},{4,0},{8,12},{12,8},{16,20},{20,16},{24,28},{28,24},{32,36},... | collective-permute-start | bytes 196616 | tf_op jit(solution)/shard_map/ppermute | solution.py:377
  30.3 11.3 %collective-permute-start.4 = (f32[128,128]{1,0:T(8,128)S(1)}, f32[128,128]{1,0:T(8,128)S(1)}, u32[]{:S(2)}, u32[]{:S(2)}) collective-permute-start(f32[128,128]{1,0:T(8,128)S(1)} %multiply_add_fusion.2), channel_id=1, source_target_pairs={{0,24},{4,28},{8,0},{12,4},{16,8},{20,12},{24,16},{28,20},{32,56},... | collective-permute-start | bytes 196616 | tf_op jit(solution)/shard_map/ppermute | solution.py:377
  33.5 8.1 %collective-permute-start.3 = (f32[128,128]{1,0:T(8,128)S(1)}, f32[128,128]{1,0:T(8,128)S(1)}, u32[]{:S(2)}, u32[]{:S(2)}) collective-permute-start(f32[128,128]{1,0:T(8,128)S(1)} %multiply_add_fusion.2), channel_id=1, source_target_pairs={{0,16},{4,20},{8,24},{12,28},{16,0},{20,4},{24,8},{28,12},{32,48},... | collective-permute-start | bytes 196616 | tf_op jit(solution)/shard_map/ppermute | solution.py:377
  34.3 7.3 %collective-permute-start.2 = (f32[128,128]{1,0:T(8,128)S(1)}, f32[128,128]{1,0:T(8,128)S(1)}, u32[]{:S(2)}, u32[]{:S(2)}) collective-permute-start(f32[128,128]{1,0:T(8,128)S(1)} %multiply_add_fusion.2), channel_id=1, source_target_pairs={{0,8},{4,12},{8,16},{12,20},{16,24},{20,28},{24,0},{28,4},{32,40},... | collective-permute-start | bytes 196616 | tf_op jit(solution)/shard_map/ppermute | solution.py:377
  35.1 11.2 %copy-start = (f32[16,1024]{1,0:T(8,128)S(1)}, f32[16,1024]{1,0:T(8,128)}, u32[]{:S(2)}) copy-start(f32[16,1024]{1,0:T(8,128)} %rates.1) | copy-start | bytes 196612
  35.1 11.2 %copy-start.1 = (f32[16,1024]{1,0:T(8,128)S(1)}, f32[16,1024]{1,0:T(8,128)}, u32[]{:S(2)}) copy-start(f32[16,1024]{1,0:T(8,128)} %residues.1) | copy-start | bytes 196612
  35.1 11.2 %copy-start.2 = (f32[1024]{0:T(1024)S(1)}, f32[1024]{0:T(1024)}, u32[]{:S(2)}) copy-start(f32[1024]{0:T(1024)} %param.9) | copy-start | bytes 12292
  41.7 7.4 %collective-permute-start.7 = (f32[128,128]{1,0:T(8,128)S(1)}, f32[128,128]{1,0:T(8,128)S(1)}, u32[]{:S(2)}, u32[]{:S(2)}) collective-permute-start(f32[128,128]{1,0:T(8,128)S(1)} %multiply_add_fusion.1), channel_id=1, source_target_pairs={{0,96},{4,100},{8,104},{12,108},{16,112},{20,116},{24,120},{28,124... | collective-permute-start | bytes 196616 | tf_op jit(solution)/shard_map/ppermute | solution.py:377
  44.7 5.8 %collective-permute-start.6 = (f32[128,128]{1,0:T(8,128)S(1)}, f32[128,128]{1,0:T(8,128)S(1)}, u32[]{:S(2)}, u32[]{:S(2)}) collective-permute-start(f32[128,128]{1,0:T(8,128)S(1)} %multiply_add_fusion.1), channel_id=1, source_target_pairs={{0,64},{4,68},{8,72},{12,76},{16,80},{20,84},{24,88},{28,92},{32,9... | collective-permute-start | bytes 196616 | tf_op jit(solution)/shard_map/ppermute | solution.py:377
  45.4 5.8 %collective-permute-start.5 = (f32[128,128]{1,0:T(8,128)S(1)}, f32[128,128]{1,0:T(8,128)S(1)}, u32[]{:S(2)}, u32[]{:S(2)}) collective-permute-start(f32[128,128]{1,0:T(8,128)S(1)} %multiply_add_fusion.1), channel_id=1, source_target_pairs={{0,32},{4,36},{8,40},{12,44},{16,48},{20,52},{24,56},{28,60},{32,6... | collective-permute-start | bytes 196616 | tf_op jit(solution)/shard_map/ppermute | solution.py:377
